TPU v7x, 256 devices: a whole 4x4x8 slice. The times are simulated.
256 devices in a mesh: row: 32 (over x, y, z_lo), col: 8 (over z_hi, core).
Axes of the slice: x: 4, y: 4, z: 8 (z_hi: 4, z_lo: 2; z = z_hi * 2 + z_lo), core: 2. Of those that a mesh axis runs over, the one named last changes fastest.
Arguments:
- features: float32 [65536, 256], P(('row', 'col')), may hold values from -6 to 6
- pre_act: float32 [65536, 256], P(('row', 'col')), may hold values from -6 to 6
- upstream: float32 [65536, 256], P(('row', 'col')), may hold values from -6 to 6
- weight: float32 [256, 256], replicated, may hold values from -0.375 to 0.375
- tile_vals: float32 [43520, 128, 128], P(('row', 'col')), may hold values from 0 to 0.046875
- tile_row: int32 [43520], P(('row', 'col')), may hold values from 0 to 15
- tile_col: int32 [43520], P(('row', 'col')), may hold values from 0 to 63
- tile_count: int32 [256], P(('row', 'col')), may hold values from 21 to 170, as said below
Outputs:
- grad_features: float32 [65536, 256], P(('row', 'col'))
- grad_weight: float32 [256, 256], replicated
Inputs may be any that keep to these rules, and one draw needn't show every extreme that they name: `tile_count`: each device holds 170, // 2, // 4 or // 8 live tiles; some device holds exactly 170.
All inputs are finite; a program needn't handle non-finite values.
Results may differ from a plain program's by a relative error of at most 0.0003.
Values sent between devices are 32-bit elements; how exact they have to be, the bound alone decides.
A program may use at most 128 MiB of HBM per device.

v0:
```python
import math

import jax
import jax.numpy as jnp
from jax import lax
from jax.sharding import PartitionSpec as P


def on_device(features, pre_act, upstream, weight, tile_vals, tile_row, tile_col, tile_count):
    tile_size = tile_vals.shape[1]
    width = features.shape[1]
    node_rows = features.shape[0]
    slots = tile_row.shape[0]
    gate_sig = jax.nn.sigmoid(pre_act)
    grad_pre = upstream * gate_sig * (1.0 + pre_act * (1.0 - gate_sig))
    gathered = lax.all_gather(grad_pre, "col", axis=0, tiled=True)
    blocks = gathered.reshape(gathered.shape[0] // tile_size, tile_size, width)
    col_tiles = lax.axis_size("row") * node_rows // tile_size
    live_slots = jnp.arange(slots) < tile_count[0]
    picked = blocks[tile_row]
    products = jnp.einsum("kab,kaf->kbf", tile_vals, picked, precision=lax.Precision.HIGHEST)
    products = products * live_slots.astype(jnp.float32)[:, None, None]
    partial_value = jax.ops.segment_sum(products, tile_col, num_segments=col_tiles).reshape(
        col_tiles * tile_size, width
    )
    aggregated = lax.psum_scatter(partial_value, "row", scatter_dimension=0, tiled=True)
    grad_features = jnp.dot(aggregated, weight.T, precision=lax.Precision.HIGHEST)
    local_grad = jnp.dot(features.T, aggregated, precision=lax.Precision.HIGHEST)
    total_nodes = node_rows * lax.axis_size("row") * lax.axis_size("col")
    summed_grad = lax.psum(local_grad, ("row", "col"))
    grad_weight = summed_grad * (1.0 / math.sqrt(total_nodes))
    return (grad_features, grad_weight)


def solution(mesh):
    return jax.shard_map(
        on_device,
        mesh=mesh,
        in_specs=(
            P(("row", "col"), None),
            P(("row", "col"), None),
            P(("row", "col"), None),
            P(),
            P(("row", "col"), None, None),
            P(("row", "col")),
            P(("row", "col")),
            P(("row", "col")),
        ),
        out_specs=(P(("row", "col"), None), P()),
        check_vma=False,
    )
```

profile of v0, /device:TPU:1, one launch (start us, length us, event | category | flops | bytes accessed | tf_op | source)
XLA Modules:
  0.0 647.4 jit_solution(4290865992502016122)
XLA Ops:
  7.2 0.0 copy-start
  7.2 0.0 all-gather.2.cloned.1.call-start
  7.2 1.9 add_multiply_fusion
  9.1 0.0 all-gather.2.cloned.1.call-update
  9.1 0.0 reduce-scatter.2.cloned.1.call-start
  9.8 0.7 compare_select_fusion
  10.5 40.7 %all-gather.2.cloned.1.call-done = f32[2048,256]{1,0:T(8,128)} async-done(((f32[256,256]{1,0:T(8,128)}), f32[2048,256]{1,0:T(8,128)}) %all-gather.2.cloned.1.call-update) | async-done | bytes 2097168 | tf_op jit(solution)/shard_map/all_gather | solution.py:16
  51.2 13.1 %gather_fusion = f32[170,128,256]{2,1,0:T(8,128)} fusion(f32[16,128,256]{2,1,0:T(8,128)} %bitcast.14, s32[1024]{0:T(1024)S(1)} %pad_clamp_fusion), kind=kCustom, calls=%fused_computation | custom fusion | bytes 44565160 | tf_op jit(solution)/shard_map/gather | solution.py:20
  64.3 46.7 %multiply_bitcast_fusion = f32[170,128,256]{1,2,0:T(8,128)} fusion(f32[170]{0:T(256)S(1)} %compare_convert_fusion, f32[170,128,256]{2,1,0:T(8,128)} %gather_fusion, f32[170,128,128]{2,1,0:T(8,128)} %param.12), kind=kOutput, calls=%fused_computation.2 | convolution fusion | flops 8561950720 | bytes 55706280 | tf_op jit(solution)/shard_map/kab,kaf->kbf/dot_general | solution.py:21
  111.0 22.4 %copy.13 = f32[170,128,256]{2,1,0:T(8,128)} copy(f32[170,128,256]{1,2,0:T(8,128)} %multiply_bitcast_fusion) | data formatting | bytes 44564480 | tf_op jit(solution)/shard_map/mul | solution.py:22
  133.3 4.4 broadcast_in_dim.10
  137.7 0.0 copy-done.2
  137.7 52.6 %scatter_fusion = f32[64,128,256]{2,1,0:T(8,128)} fusion(f32[64,128,256]{2,1,0:T(8,128)} %broadcast_in_dim.10, s32[170]{0:T(256)S(1)} %copy-done.2, f32[170,128,256]{2,1,0:T(8,128)} %copy.13), kind=kCustom, calls=%fused_computation.1 | custom fusion | flops 5570560 | bytes 66847400 | tf_op jit(solution)/shard_map/scatter-add | solution.py:23
  190.3 0.0 reduce-scatter.2.cloned.1.call-update
  190.3 0.0 all-reduce.2.cloned.1.call-start
  190.4 180.5 %reduce-scatter.2.cloned.1.call-done = f32[256,256]{1,0:T(8,128)} async-done(((f32[8192,256]{1,0:T(8,128)}), f32[256,256]{1,0:T(8,128)}) %reduce-scatter.2.cloned.1.call-update) | async-done | bytes 262160 | tf_op jit(solution)/shard_map/reduce_scatter | solution.py:26
  370.9 0.0 copy-done
  370.9 2.2 convolution_bitcast_fusion
  373.2 0.0 all-reduce.2.cloned.1.call-update
  373.2 0.0 copy-done.1
  373.2 2.1 fusion
  375.3 263.9 %all-reduce.2.cloned.1.call-done = f32[256,256]{0,1:T(8,128)} async-done(((f32[256,256]{0,1:T(8,128)}), f32[256,256]{0,1:T(8,128)}) %all-reduce.2.cloned.1.call-update) | async-done | bytes 262160 | tf_op jit(solution)/shard_map/psum | solution.py:30
  639.1 1.0 broadcast_multiply_fusion
  640.1 0.8 copy.14
  (4 shorter events, 0.0 us)
Async XLA Ops:
  7.2 363.7 %copy-start = (f32[256,256]{1,0:T(8,128)S(1)}, f32[256,256]{1,0:T(8,128)}, u32[]{:S(2)}) copy-start(f32[256,256]{1,0:T(8,128)} %param.8) | copy-start | bytes 786436
  7.2 44.0 %all-gather.2.cloned.1.call-start = ((), (), s32[]{:S(2)}) async-start(), calls=%async_computation.1 | async-start | bytes 2359296 | tf_op jit(solution)/shard_map/all_gather | solution.py:16
  9.1 361.8 %reduce-scatter.2.cloned.1.call-start = ((), (), s32[]{:S(2)}) async-start(), calls=%async_computation.2 | async-start | bytes 8650752 | tf_op jit(solution)/shard_map/reduce_scatter | solution.py:26
  111.0 26.7 %copy-start.2 = (s32[170]{0:T(256)S(1)}, s32[170]{0:T(256)}, u32[]{:S(2)}) copy-start(s32[170]{0:T(256)} %param.14) | copy-start | bytes 2044
  137.7 235.5 %copy-start.1 = (f32[256,256]{1,0:T(8,128)S(1)}, f32[256,256]{1,0:T(8,128)}, u32[]{:S(2)}) copy-start(f32[256,256]{1,0:T(8,128)} %param.11) | copy-start | bytes 786436
  190.3 448.8 %all-reduce.2.cloned.1.call-start = ((), (), s32[]{:S(2)}) async-start(), calls=%async_computation.3 | async-start | bytes 524288 | tf_op jit(solution)/shard_map/psum | solution.py:30
Sparse Core Ops, SparseCore 0:
  10.4 40.7 all-gather.1
  190.5 180.4 reduce-scatter.1
  376.9 262.1 all-reduce.1
where the time goes:
time: 649 us; the launch traced here: 647 us
  waiting for transfers between devices  485 us (75%)
  other arithmetic  56.1 us (9%)
  matrix products  51 us (8%)
  local copies, waits for them, and re-layouts  40.7 us (6%)
  between operations  14.4 us (2%)
    psum x1, waiting for transfers between devices, on_device(): summed_grad = lax.psum(local_grad, ('row', 'col'))  264 us
    reduce_scatter x1, waiting for transfers between devices, on_device(): lax.psum_scatter(partial_value, 'row', scatter_dimension=0, tiled=True)  181 us
    scatter-add x1, other arithmetic, on_device(): jax.ops.segment_sum(products, tile_col, num_segments=col_tiles)  52.6 us
    dot_general x1, matrix products, on_device(): jnp.einsum('kab,kaf->kbf', tile_vals, picked, precision=lax.Precision.HIG...  46.7 us
    all_gather x1, waiting for transfers between devices, on_device(): gathered = lax.all_gather(grad_pre, 'col', axis=0, tiled=True)  40.7 us
    mul x1, local copies, waits for them, and re-layouts, on_device(): products = products * live_slots.astype(jnp.float32)[:, None, None]  22.4 us
    gather x1, local copies, waits for them, and re-layouts, on_device(): picked = blocks[tile_row]  13.1 us
  transfers between devices with their start and end apart: 3, of which 3 were waited for; matrix products, arithmetic and copies ran while one was open for 0% of the time, Pallas kernels for 0%

commit v1 on v0

v1 whole, which is shorter than its diff:
```python
import functools
import math

import jax
import jax.numpy as jnp
from jax import lax
from jax.experimental import pallas as pl
from jax.experimental.pallas import tpu as pltpu
from jax.sharding import PartitionSpec as P

MESH = pl.DeviceIdType.MESH
HIGH = lax.Precision.HIGHEST


def place():
    row = lax.axis_index("row")
    col = lax.axis_index("col")
    return row // 8, (row // 2) % 4, row % 2, col // 2, col % 2


def device(x, y, zl, zh, core):
    return (x * 8 + y * 2 + zl, zh * 2 + core)


def copy_to(src, dst, send, recv, target):
    return pltpu.make_async_remote_copy(
        src_ref=src, dst_ref=dst, send_sem=send, recv_sem=recv, device_id=target, device_id_type=MESH
    )


def greet(peers):
    barrier = pltpu.get_barrier_semaphore()
    for peer in peers:
        pl.semaphore_signal(barrier, inc=1, device_id=peer, device_id_type=MESH)
    pl.semaphore_wait(barrier, len(peers))


def gather_kernel(pre_ref, up_ref, gt_ref, send, recv):
    x, y, zl, zh, core = place()
    right = device(x, y, zl, (zh + 1) % 4, core)
    left = device(x, y, zl, (zh + 3) % 4, core)
    sibling = device(x, y, zl, zh, 1 - core)
    greet((right, left, sibling))
    pre = pre_ref[...]
    gate = jax.nn.sigmoid(pre)
    grad = up_ref[...] * gate * (1.0 + pre * (1.0 - gate))
    for t in range(2):
        gt_ref[zh * 4 + core * 2 + t] = grad[t * 128:(t + 1) * 128, :].T

    def part(block_zh, half):
        return gt_ref.at[pl.ds(block_zh * 4 + core * 2, 2), pl.ds(half * 128, 128), :]

    me, after, before, far = zh, (zh + 1) % 4, (zh + 3) % 4, (zh + 2) % 4
    started = []

    def go(ref, slot, target):
        copy = copy_to(ref, ref, send.at[slot], recv.at[slot], target)
        copy.start()
        started.append(copy)

    def arrived(ref, slot):
        copy_to(ref, ref, send.at[slot], recv.at[slot], right).wait_recv()

    go(part(me, 0), 0, right)
    go(part(me, 1), 3, left)
    go(part(me, 1), 1, right)
    go(part(me, 0), 2, left)
    go(part(me, 0), 6, sibling)
    go(part(me, 1), 7, sibling)
    arrived(part(before, 0), 0)
    go(part(before, 0), 4, right)
    arrived(part(after, 1), 3)
    go(part(after, 1), 5, left)
    go(part(before, 0), 8, sibling)
    go(part(after, 1), 9, sibling)
    arrived(part(before, 1), 1)
    go(part(before, 1), 10, sibling)
    arrived(part(after, 0), 2)
    go(part(after, 0), 11, sibling)
    arrived(part(far, 0), 4)
    go(part(far, 0), 12, sibling)
    arrived(part(far, 1), 5)
    go(part(far, 1), 13, sibling)
    other = 1 - core

    def mirrored(block_zh, half):
        return gt_ref.at[pl.ds(block_zh * 4 + other * 2, 2), pl.ds(half * 128, 128), :]

    for slot, (block, half) in zip(
        range(6, 14),
        ((me, 0), (me, 1), (before, 0), (after, 1), (before, 1), (after, 0), (far, 0), (far, 1)),
    ):
        arrived(mirrored(block, half), slot)
    for copy in started:
        copy.wait_send()


def gathered(pre_act, upstream):
    return pl.pallas_call(
        gather_kernel,
        out_shape=jax.ShapeDtypeStruct((16, 256, 128), jnp.float32),
        in_specs=[pl.BlockSpec(memory_space=pltpu.VMEM)] * 2,
        out_specs=pl.BlockSpec(memory_space=pltpu.VMEM),
        scratch_shapes=[pltpu.SemaphoreType.DMA((14,)), pltpu.SemaphoreType.DMA((14,))],
        compiler_params=pltpu.CompilerParams(collective_id=0, has_side_effects=True),
        name="gather",
    )(pre_act, upstream)


def split(value):
    high = value.astype(jnp.bfloat16)
    return high, (value - high.astype(jnp.float32)).astype(jnp.bfloat16)


STEP = 10


def tiles_kernel(rows, cols, count, gt_ref, tiles_ref, out_ref, parts):
    step = pl.program_id(0)

    @pl.when(step == 0)
    def _():
        @pl.loop(0, 64)
        def _(i):
            out_ref[i] = jnp.zeros((256, 128), jnp.float32)

        @pl.loop(0, 16)
        def _(i):
            high, low = split(gt_ref[i])
            parts[i, :, :128] = high
            parts[i, :, 128:] = low

    for j in range(STEP):
        k = step * STEP + j

        @pl.when(k < count[0])
        def _():
            high, low = split(tiles_ref[j])
            both = jnp.concatenate([high, low], axis=1)
            both = jnp.concatenate([both, both], axis=0)
            product = jnp.dot(parts[rows[k]], both, preferred_element_type=jnp.float32)
            out_ref[cols[k]] += product[:, :128] + product[:, 128:]


def tile_sums(tile_row, tile_col, tile_count, gt, tile_vals):
    slots = tile_vals.shape[0]
    return pl.pallas_call(
        tiles_kernel,
        out_shape=jax.ShapeDtypeStruct((64, 256, 128), jnp.float32),
        grid_spec=pltpu.PrefetchScalarGridSpec(
            num_scalar_prefetch=3,
            grid=(slots // STEP,),
            in_specs=[
                pl.BlockSpec(memory_space=pltpu.VMEM),
                pl.BlockSpec((STEP, 128, 128), lambda i, *_: (i, 0, 0)),
            ],
            out_specs=pl.BlockSpec(memory_space=pltpu.VMEM),
            scratch_shapes=[pltpu.VMEM((16, 256, 256), jnp.bfloat16)],
        ),
        compiler_params=pltpu.CompilerParams(vmem_limit_bytes=48 << 20),
        name="tiles",
    )(tile_row, tile_col, tile_count, gt, tile_vals)


def scatter_kernel(p_ref, agg_ref, r1, r2a, r2b, x1, s1, s2a, s2b, x2, zbuf, *sems):
    x, y, zl, zh, core = place()
    (r1s, r1r, r2as, r2ar, r2bs, r2br, s1s, s1r, s2as, s2ar, s2bs, s2br, zs, zr) = sems
    x_side = (device((x + 1) % 4, y, zl, zh, core), device((x + 3) % 4, y, zl, zh, core))
    y_side = (device(x, (y + 1) % 4, zl, zh, core), device(x, (y + 3) % 4, zl, zh, core))
    z_side = device(x, y, 1 - zl, zh, core)
    greet(x_side + y_side + (z_side,))
    first = (x_side, y_side)
    second = (y_side, x_side)
    c1 = (x, y)
    c2 = (y, x)
    order = (2, 1, 3, 0)
    sides = tuple((h, d) for h in range(2) for d in range(2))
    ahead = (1, 3)

    def block(h, d1, p, q):
        d1 = (c1[h] + d1) % 4
        d2 = (c2[h] + order[p]) % 4
        rows = pl.ds(h * 128 + q * 64, 64)
        return p_ref.at[d1, d2, :, rows, :] if h == 0 else p_ref.at[d2, d1, :, rows, :]

    started = []

    def go(src, dst, send, recv, target):
        copy = copy_to(src, dst, send, recv, target)
        copy.start()
        started.append(copy)
        return copy

    def arrived(dst, send, recv):
        copy_to(dst, dst, send, recv, z_side).wait_recv()

    for p in range(4):
        for h, d in sides:
            go(block(h, 2, p, d), r1.at[h, d, p], r1s.at[h, d, p], r1r.at[h, d, p], first[h][d])
    for p in range(4):
        for h, d in sides:
            arrived(r1.at[h, d, p], r1s.at[h, d, p], r1r.at[h, d, p])
            r1[h, d, p] += block(h, ahead[d], p, d)[...]
            go(r1.at[h, d, p], r2b.at[h, d, p], r2bs.at[h, d, p], r2br.at[h, d, p], first[h][d])
            go(block(h, ahead[d], p, 1 - d), r2a.at[h, d, p], r2as.at[h, d, p], r2ar.at[h, d, p], first[h][d])
    for p in range(4):
        for h in range(2):
            for d in range(2):
                arrived(r2a.at[h, d, p], r2as.at[h, d, p], r2ar.at[h, d, p])
                arrived(r2b.at[h, d, p], r2bs.at[h, d, p], r2br.at[h, d, p])
            for q in range(2):
                x1[h, p, q] = block(h, 0, p, q)[...] + r2b[h, q, p] + r2a[h, 1 - q, p]
            if p == 0:
                for d in range(2):
                    go(x1.at[h, 0, d], s1.at[h, d], s1s.at[h, d], s1r.at[h, d], second[h][d])
            elif p < 3:
                d = p - 1
                go(x1.at[h, p, 1 - d], s2a.at[h, d], s2as.at[h, d], s2ar.at[h, d], second[h][d])
                arrived(s1.at[h, d], s1s.at[h, d], s1r.at[h, d])
                x1[h, p, d] += s1[h, d]
                go(x1.at[h, p, d], s2b.at[h, d], s2bs.at[h, d], s2br.at[h, d], second[h][d])
    for h in range(2):
        for d in range(2):
            arrived(s2a.at[h, d], s2as.at[h, d], s2ar.at[h, d])
            arrived(s2b.at[h, d], s2bs.at[h, d], s2br.at[h, d])
        for q in range(2):
            x2[h, q] = x1[h, 3, q] + s2b[h, q] + s2a[h, 1 - q]
        go(x2.at[h, :, pl.ds(2 - 2 * zl, 2)], zbuf.at[h], zs.at[h], zr.at[h], z_side)
    for h in range(2):
        arrived(zbuf.at[h], zs.at[h], zr.at[h])
        for q in range(2):
            agg_ref[:, h * 128 + q * 64:h * 128 + q * 64 + 64, :] = (
                x2[h, q, pl.ds(2 * zl, 2)] + zbuf[h, q]
            )
    for copy in started:
        copy.wait_send()


def scattered(partial_sums):
    piece = (4, 64, 128)
    f32 = jnp.float32
    dma = pltpu.SemaphoreType.DMA
    return pl.pallas_call(
        scatter_kernel,
        out_shape=jax.ShapeDtypeStruct((2, 256, 128), f32),
        in_specs=[pl.BlockSpec(memory_space=pltpu.VMEM)],
        out_specs=pl.BlockSpec(memory_space=pltpu.VMEM),
        scratch_shapes=[
            pltpu.VMEM((2, 2, 4) + piece, f32),
            pltpu.VMEM((2, 2, 4) + piece, f32),
            pltpu.VMEM((2, 2, 4) + piece, f32),
            pltpu.VMEM((2, 4, 2) + piece, f32),
            pltpu.VMEM((2, 2) + piece, f32),
            pltpu.VMEM((2, 2) + piece, f32),
            pltpu.VMEM((2, 2) + piece, f32),
            pltpu.VMEM((2, 2) + piece, f32),
            pltpu.VMEM((2, 2, 2, 64, 128), f32),
        ]
        + [dma((2, 2, 4))] * 6
        + [dma((2, 2))] * 6
        + [dma((2,))] * 2,
        compiler_params=pltpu.CompilerParams(
            collective_id=1, has_side_effects=True, vmem_limit_bytes=48 << 20
        ),
        name="scatter",
    )(partial_sums.reshape(4, 4, 4, 256, 128))


def finish_kernel(agg_ref, feat_ref, weight_ref, gf_ref, gw_ref, local, a1, part, a2, whole, s1, r1, s2, r2, s3, r3):
    x, y, zl, zh, core = place()
    me = x * 8 + y * 2 + core
    mz = zh * 2 + zl

    def plane(j):
        return device(j // 8, (j // 2) % 4, zl, zh, j % 2)

    def column(j):
        return device(x, y, j % 2, j // 2, core)

    barrier = pltpu.get_barrier_semaphore()

    @pl.loop(1, 32)
    def _(j):
        pl.semaphore_signal(barrier, inc=1, device_id=plane((me + j) % 32), device_id_type=MESH)

    @pl.loop(1, 8)
    def _(j):
        pl.semaphore_signal(barrier, inc=1, device_id=column((mz + j) % 8), device_id_type=MESH)

    grad = jnp.dot(agg_ref[0], feat_ref[:128], precision=HIGH, preferred_element_type=jnp.float32)
    grad += jnp.dot(agg_ref[1], feat_ref[128:], precision=HIGH, preferred_element_type=jnp.float32)
    local[...] = grad.reshape(32, 8, 256)
    pl.semaphore_wait(barrier, 38)

    @pl.loop(1, 32)
    def _(j):
        to = (me + j) % 32
        copy_to(local.at[to], a1.at[me], s1, r1, plane(to)).start()

    a1[me] = local[me]
    for t in range(2):
        gf_ref[:, t * 128:(t + 1) * 128] = jnp.dot(
            weight_ref[...], agg_ref[t], precision=HIGH, preferred_element_type=jnp.float32
        )
    all_but_one = pltpu.make_async_copy(a1.at[pl.ds(0, 31)], a1.at[pl.ds(0, 31)], r1)
    all_but_one.wait()
    part[...] = jnp.sum(a1[...], axis=0)

    @pl.loop(1, 8)
    def _(j):
        copy_to(part, a2.at[mz], s2, r2, column((mz + j) % 8)).start()

    a2[mz] = part[...]
    pltpu.make_async_copy(a2.at[pl.ds(0, 7)], a2.at[pl.ds(0, 7)], r2).wait()
    whole[me] = jnp.sum(a2[...], axis=0)

    @pl.loop(1, 32)
    def _(j):
        copy_to(whole.at[me], whole.at[me], s3, r3, plane((me + j) % 32)).start()

    pltpu.make_async_copy(whole.at[pl.ds(0, 31)], whole.at[pl.ds(0, 31)], r3).wait()
    gw_ref[...] = whole[...].reshape(256, 256)
    pltpu.make_async_copy(a1.at[pl.ds(0, 31)], a1.at[pl.ds(0, 31)], s1).wait()
    pltpu.make_async_copy(a2.at[pl.ds(0, 7)], a2.at[pl.ds(0, 7)], s2).wait()
    pltpu.make_async_copy(whole.at[pl.ds(0, 31)], whole.at[pl.ds(0, 31)], s3).wait()


def finished(agg, features, weight):
    f32 = jnp.float32
    dma = pltpu.SemaphoreType.DMA
    square = jax.ShapeDtypeStruct((256, 256), f32)
    return pl.pallas_call(
        finish_kernel,
        out_shape=(square, square),
        in_specs=[pl.BlockSpec(memory_space=pltpu.VMEM)] * 3,
        out_specs=(pl.BlockSpec(memory_space=pltpu.VMEM),) * 2,
        scratch_shapes=[
            pltpu.VMEM((32, 8, 256), f32),
            pltpu.VMEM((32, 8, 256), f32),
            pltpu.VMEM((8, 256), f32),
            pltpu.VMEM((8, 8, 256), f32),
            pltpu.VMEM((32, 8, 256), f32),
        ]
        + [dma] * 6,
        compiler_params=pltpu.CompilerParams(collective_id=2, has_side_effects=True),
        name="finish",
    )(agg, features, weight)


def on_device(features, pre_act, upstream, weight, tile_vals, tile_row, tile_col, tile_count):
    gt = gathered(pre_act, upstream)
    sums = tile_sums(tile_row, tile_col, tile_count, gt, tile_vals)
    agg = scattered(sums)
    gf, gw = finished(agg, features, weight)
    total_nodes = features.shape[0] * 256
    return gf.T, gw.T * (1.0 / math.sqrt(total_nodes))


def solution(mesh):
    return jax.shard_map(
        on_device,
        mesh=mesh,
        in_specs=(
            P(("row", "col"), None),
            P(("row", "col"), None),
            P(("row", "col"), None),
            P(),
            P(("row", "col"), None, None),
            P(("row", "col")),
            P(("row", "col")),
            P(("row", "col")),
        ),
        out_specs=(P(("row", "col"), None), P()),
        check_vma=False,
    )
```

time: 649 us -> 163 us (0.25)
  waiting for transfers between devices: 485 us -> 0 us
  Pallas kernels: 0 us -> 154 us
  other arithmetic: 56.1 us -> 0.97 us
  matrix products: 51 us -> 0 us
  local copies, waits for them, and re-layouts: 40.7 us -> 6.26 us
  between operations: 14.4 us -> 1.32 us
    psum x1 -> x0, waiting for transfers between devices: 264 us -> none  [on_device(): summed_grad = lax.psum(local_grad, ('row', 'col'))]
    reduce_scatter x1 -> x0, waiting for transfers between devices: 181 us -> none  [on_device(): lax.psum_scatter(partial_value, 'row', scatter_dimension=0, tiled=True)]
    pallas_call x0 -> x4, Pallas kernels: none -> 154 us  [the longest x1 79.2 us: scattered(): pl.pallas_call(scatter_kernel, out_shape=jax.ShapeDtypeStruct((2, 256, 12...]
    scatter-add x1 -> x0, other arithmetic: 52.6 us -> none  [on_device(): jax.ops.segment_sum(products, tile_col, num_segments=col_tiles)]
    dot_general x3 -> x0, matrix products: 51 us -> none  [the longest x1 46.7 us: on_device(): jnp.einsum('kab,kaf->kbf', tile_vals, picked, precision=lax.Precision.HIG...]
    all_gather x1 -> x0, waiting for transfers between devices: 40.7 us -> none  [on_device(): gathered = lax.all_gather(grad_pre, 'col', axis=0, tiled=True)]
    mul x1 -> x0, local copies, waits for them, and re-layouts: 22.4 us -> none  [on_device(): products = products * live_slots.astype(jnp.float32)[:, None, None]]
    gather x1 -> x0, local copies, waits for them, and re-layouts: 13.1 us -> none  [on_device(): picked = blocks[tile_row]]
  transfers between devices with their start and end apart: 3 -> 0, of which waited for: 3 -> 0; matrix products, arithmetic and copies ran while one was open for 0% -> 0% of each run, Pallas kernels for 0% -> 0%
where the time goes in v1:
time: 163 us; the launch traced here: 162 us
  Pallas kernels  154 us (94%)
  local copies, waits for them, and re-layouts  6.26 us (4%)
    pallas_call x1, Pallas kernels, scattered(): pl.pallas_call(scatter_kernel, out_shape=jax.ShapeDtypeStruct((2, 256, 12...  79.2 us
    pallas_call x1, Pallas kernels, gathered(): pl.pallas_call(gather_kernel, out_shape=jax.ShapeDtypeStruct((16, 256, 12...  30.2 us
    pallas_call x1, Pallas kernels, finished(): pl.pallas_call(finish_kernel, out_shape=(square, square), in_specs=[pl.Bl...  26.5 us
    pallas_call x1, Pallas kernels, tile_sums(): pl.pallas_call(tiles_kernel, out_shape=jax.ShapeDtypeStruct((64, 256, 128...  18 us
    unnamed x10, local copies, waits for them, and re-layouts  6.26 us

profile of v1, /device:TPU:1, one launch (start us, length us, event | category | flops | bytes accessed | tf_op | source)
XLA Modules:
  0.0 162.5 jit_solution(10015255684745740055)
XLA Ops:
  1.3 30.2 %gather.1.gt_ref = f32[16,256,128]{2,1,0:T(8,128)} custom-call(f32[256,256]{1,0:T(8,128)} %pre_ref.1, f32[256,256]{1,0:T(8,128)} %up_ref.1), custom_call_target="tpu_custom_call" | custom-call | tf_op jit(solution)/shard_map/gather/pallas_call | solution.py:99
  31.4 0.0 copy-start
  31.5 1.6 copy-done
  33.0 0.0 copy-start.2
  33.0 0.7 copy-done.2
  33.7 0.0 copy-start.3
  33.7 0.7 copy-done.3
  34.4 18.0 %tiles.1 = f32[64,256,128]{2,1,0:T(8,128)} custom-call(s32[170]{0:T(256)S(1)} %copy-done.2, s32[170]{0:T(256)S(1)} %copy-done.3, s32[1]{0:T(128)S(6)} %copy.12.count, f32[16,256,128]{2,1,0:T(8,128)S(1)} %copy-done, f32[170,128,128]{2,1,0:T(8,128)} %tiles_ref.1), custom_call_target="tpu_custom_call" | custom-call | tf_op jit(solution)/shard_map/tiles/pallas_call | solution.py:147
  52.4 79.2 %scatter.1.agg_ref = f32[2,256,128]{2,1,0:T(8,128)S(1)} custom-call(f32[4,4,4,256,128]{4,3,2,1,0:T(8,128)} %bitcast.4), custom_call_target="tpu_custom_call" | custom-call | tf_op jit(solution)/shard_map/scatter/pallas_call | solution.py:243
  131.7 0.0 copy-start.1
  131.7 0.7 copy-done.1
  132.4 26.5 %finish.1 = (f32[256,256]{1,0:T(8,128)}, f32[256,256]{1,0:T(8,128)}) custom-call(f32[2,256,128]{2,1,0:T(8,128)} %copy-done.1, f32[256,256]{1,0:T(8,128)} %feat_ref.1, f32[256,256]{1,0:T(8,128)} %weight_ref.1), custom_call_target="tpu_custom_call" | custom-call | tf_op jit(solution)/shard_map/finish/pallas_call | solution.py:332
  158.9 1.8 %copy.10 = f32[256,256]{1,0:T(8,128)} copy(f32[256,256]{0,1:T(8,128)} %bitcast.5) | data formatting | bytes 524288
  160.6 1.0 multiply_bitcast_fusion
  161.6 0.8 copy.11
Async XLA Ops:
  31.4 1.6 copy-start
  33.0 0.7 copy-start.2
  33.7 0.7 copy-start.3
  131.7 0.7 copy-start.1

commit v2 on v0

v2 whole, which is shorter than its diff:
```python
import math

import jax
import jax.numpy as jnp
from jax import lax
from jax.experimental import pallas as pl
from jax.experimental.pallas import tpu as pltpu
from jax.sharding import PartitionSpec as P

MESH = pl.DeviceIdType.MESH
HIGH = lax.Precision.HIGHEST
F32 = jnp.float32
BF16 = jnp.bfloat16
SLOTS = 170
UNROLL = 34
LOADS = 10


def place():
    row = lax.axis_index("row")
    col = lax.axis_index("col")
    return row // 8, (row // 2) % 4, row % 2, col // 2, col % 2


def device(x, y, zl, zh, core):
    return (x * 8 + y * 2 + zl, zh * 2 + core)


def copy_to(src, dst, send, recv, target):
    return pltpu.make_async_remote_copy(
        src_ref=src, dst_ref=dst, send_sem=send, recv_sem=recv, device_id=target, device_id_type=MESH
    )


def split(value):
    high = value.astype(BF16)
    return high, (value - high.astype(F32)).astype(BF16)


def dot(a, b):
    return jnp.dot(a, b, precision=HIGH, preferred_element_type=F32)


def kernel(
    pre_ref, up_ref, feat_ref, weight_ref, row_ref, col_ref, count_ref, tiles_hbm,
    gf_ref, gw_ref,
    tiles, runs, parts, gt, sums, r1, r2a, r2b, x1, s1, s2a, s2b, x2, zbuf, agg, local, a1, part, a2,
    raw, table_v, table,
    load_sem, table_sem, ag_s, ag_r, r1s, r1r, r2as, r2ar, r2bs, r2br, s1s, s1r, s2as, s2ar, s2bs, s2br, zs, zr,
    w1s, w1r, w2s, w2r, w3s, w3r,
):
    x, y, zl, zh, core = place()
    me = x * 8 + y * 2 + core
    mz = zh * 2 + zl
    here = zh * 4 + core * 2

    def plane(j):
        return device(j // 8, (j // 2) % 4, zl, zh, j % 2)

    def column(j):
        return device(x, y, j % 2, j // 2, core)

    barrier = pltpu.get_barrier_semaphore()

    @pl.loop(1, 32)
    def _(j):
        pl.semaphore_signal(barrier, inc=1, device_id=plane((me + j) % 32), device_id_type=MESH)

    @pl.loop(1, 8)
    def _(j):
        pl.semaphore_signal(barrier, inc=1, device_id=column((mz + j) % 8), device_id_type=MESH)

    per_load = SLOTS // LOADS
    loads = []
    for i in range(LOADS):
        rows = pl.ds(i * per_load, per_load)
        loads.append(pltpu.make_async_copy(tiles_hbm.at[rows], tiles.at[rows], load_sem.at[i]))
        loads[-1].start()

    pre = pre_ref[...]
    gate = jax.nn.sigmoid(pre)
    grad = up_ref[...] * gate * (1.0 + pre * (1.0 - gate))
    for t in range(2):
        turned = grad[t * 128:(t + 1) * 128, :].T
        for h in range(2):
            gt[h, here + t] = turned[h * 128:(h + 1) * 128]
    pl.semaphore_wait(barrier, 38)

    started = []

    def go(src, dst, send, recv, target):
        copy = copy_to(src, dst, send, recv, target)
        copy.start()
        started.append(copy)

    z_right = device(x, y, zl, (zh + 1) % 4, core)
    z_left = device(x, y, zl, (zh + 3) % 4, core)
    sibling = device(x, y, zl, zh, 1 - core)
    z_side = device(x, y, 1 - zl, zh, core)
    x_side = (device((x + 1) % 4, y, zl, zh, core), device((x + 3) % 4, y, zl, zh, core))
    y_side = (device(x, (y + 1) % 4, zl, zh, core), device(x, (y + 3) % 4, zl, zh, core))

    def arrived(dst, send, recv):
        copy_to(dst, dst, send, recv, z_side).wait_recv()

    after, before, far = (zh + 1) % 4, (zh + 3) % 4, (zh + 2) % 4

    def block(h, block_zh, block_core, quarter):
        return gt.at[h, pl.ds(block_zh * 4 + block_core * 2, 2), pl.ds(quarter * 64, 64), :]

    def pass_on(h, block_zh, quarter, slot, target):
        ref = block(h, block_zh, core, quarter)
        go(ref, ref, ag_s.at[h, slot], ag_r.at[h, slot], target)

    def came(h, block_zh, block_core, quarter, slot):
        arrived(block(h, block_zh, block_core, quarter), ag_s.at[h, slot], ag_r.at[h, slot])

    def gather_own(h):
        pass_on(h, zh, 0, 0, z_right)
        pass_on(h, zh, 1, 3, z_left)
        pass_on(h, zh, 1, 1, z_right)
        pass_on(h, zh, 0, 2, z_left)
        pass_on(h, zh, 0, 6, sibling)
        pass_on(h, zh, 1, 7, sibling)

    def gather_next(h):
        came(h, before, core, 0, 0)
        pass_on(h, before, 0, 4, z_right)
        came(h, after, core, 1, 3)
        pass_on(h, after, 1, 5, z_left)
        pass_on(h, before, 0, 8, sibling)
        pass_on(h, after, 1, 9, sibling)
        came(h, before, core, 1, 1)
        pass_on(h, before, 1, 10, sibling)
        came(h, after, core, 0, 2)
        pass_on(h, after, 0, 11, sibling)

    def gather_last(h):
        came(h, far, core, 0, 4)
        pass_on(h, far, 0, 12, sibling)
        came(h, far, core, 1, 5)
        pass_on(h, far, 1, 13, sibling)
        blocks = ((zh, 0), (zh, 1), (before, 0), (after, 1), (before, 1), (after, 0), (far, 0), (far, 1))
        for i, (block_zh, quarter) in enumerate(blocks):
            came(h, block_zh, 1 - core, quarter, 6 + i)

    def sort_tiles():
        raw[...] = jnp.zeros((8, 256), jnp.int32)
        raw[0:1, 0:SLOTS] = col_ref[...]
        raw[1:2, 0:SLOTS] = row_ref[...]
        lane = lax.broadcasted_iota(jnp.int32, (8, 256), 1)
        across = lax.broadcasted_iota(jnp.int32, (256, 256), 1)
        slot_down = lax.broadcasted_iota(jnp.int32, (256, 1), 0)
        one, none = jnp.int32(1), jnp.int32(0)

        def down(value):
            return jnp.broadcast_to(value, (8, 256)).T[:, 0:1]

        def total(value):
            return jnp.sum(value, axis=0, keepdims=True)

        def within(value, last):
            return jnp.minimum(jnp.maximum(value, 0), last)

        values = raw[...]
        cols = jnp.where(lane < count_ref[0], values[0:1], 64)
        key = cols * 256 + lane
        rank = down(total(jnp.where(down(key[0:1]) < key[0:1], one, none)))
        col_down, row_down = down(cols[0:1]), down(values[1:2])
        at = rank == across
        next_at = rank + 1 == across
        sorted_cols = total(jnp.where(at, col_down, 0))
        previous = total(jnp.where(next_at, col_down + 1, 0)) - 1
        table_v[0:1] = within(total(jnp.where(at, slot_down, 0)), SLOTS - 1)
        table_v[1:2] = within(total(jnp.where(at, row_down, 0)), 15)
        table_v[2:3] = jnp.where(sorted_cols == previous, one, none)
        table_v[3:4] = within(total(jnp.where(col_down <= across, one, none)), SLOTS)
        table_v[4:5] = jnp.where(total(jnp.where(col_down == across, one, none)) > 0, one, none)
        table_v[5:8] = jnp.zeros((3, 256), jnp.int32)
        copy = pltpu.make_async_copy(table_v, table, table_sem)
        copy.start()
        copy.wait()

    def products(h):
        @pl.loop(0, 16)
        def _(i):
            high, low = split(gt[h, i])
            parts[i, :, :128] = high
            parts[i, :, 128:] = low

        @pl.loop(0, SLOTS // UNROLL)
        def _(i):
            for j in range(UNROLL):
                k = i * UNROLL + j
                high, low = split(tiles[table[0, k]])
                both = jnp.concatenate([high, low], axis=1)
                both = jnp.concatenate([both, both], axis=0)
                product = jnp.dot(parts[table[1, k]], both, preferred_element_type=F32)
                carried = table[2, k].astype(F32) * runs[k]
                runs[k + 1] = carried + product[:, :128] + product[:, 128:]

        @pl.loop(0, 16)
        def _(i):
            for j in range(4):
                t = i * 4 + j
                sums[h, i // 4, i % 4, j] = table[4, t].astype(F32) * runs[table[3, t]]

    first, second = (x_side, y_side), (y_side, x_side)
    c1, c2 = (x, y), (y, x)
    order = (2, 1, 3, 0)
    ahead = (1, 3)
    sides = tuple((a, d) for a in range(2) for d in range(2))

    def piece(h, a, d1, p, q):
        d1 = (c1[a] + d1) % 4
        d2 = (c2[a] + order[p]) % 4
        rows = pl.ds(a * 64 + q * 32, 32)
        return sums.at[h, d1, d2, :, rows, :] if a == 0 else sums.at[h, d2, d1, :, rows, :]

    def scatter_start(h):
        for p in range(4):
            for a, d in sides:
                i = (h, a, d, p)
                go(piece(h, a, 2, p, d), r1.at[i], r1s.at[i], r1r.at[i], first[a][d])

    def scatter_direct(h):
        for p in range(4):
            for a, d in sides:
                i = (h, a, d, p)
                go(piece(h, a, ahead[d], p, 1 - d), r2a.at[i], r2as.at[i], r2ar.at[i], first[a][d])

    def scatter_ring(h):
        for p in range(4):
            for a, d in sides:
                i = (h, a, d, p)
                arrived(r1.at[i], r1s.at[i], r1r.at[i])
                r1[i] += piece(h, a, ahead[d], p, d)[...]
                go(r1.at[i], r2b.at[i], r2bs.at[i], r2br.at[i], first[a][d])

    def scatter_cross(h, p):
        for a in range(2):
            for d in range(2):
                i = (h, a, d, p)
                arrived(r2a.at[i], r2as.at[i], r2ar.at[i])
                arrived(r2b.at[i], r2bs.at[i], r2br.at[i])
            for q in range(2):
                x1[h, a, p, q] = piece(h, a, 0, p, q)[...] + r2b[h, a, q, p] + r2a[h, a, 1 - q, p]
            if p == 0:
                for d in range(2):
                    i = (h, a, d)
                    go(x1.at[h, a, 0, d], s1.at[i], s1s.at[i], s1r.at[i], second[a][d])
            elif p < 3:
                i = (h, a, p - 1)
                go(x1.at[h, a, p, 2 - p], s2a.at[i], s2as.at[i], s2ar.at[i], second[a][p - 1])

    def scatter_cross_ring(h):
        for p in (1, 2):
            for a in range(2):
                i = (h, a, p - 1)
                arrived(s1.at[i], s1s.at[i], s1r.at[i])
                x1[h, a, p, p - 1] += s1[i]
                go(x1.at[h, a, p, p - 1], s2b.at[i], s2bs.at[i], s2br.at[i], second[a][p - 1])

    def scatter_z(h):
        for a in range(2):
            for d in range(2):
                i = (h, a, d)
                arrived(s2a.at[i], s2as.at[i], s2ar.at[i])
                arrived(s2b.at[i], s2bs.at[i], s2br.at[i])
            for q in range(2):
                x2[h, a, q] = x1[h, a, 3, q] + s2b[h, a, q] + s2a[h, a, 1 - q]
            i = (h, a)
            go(x2.at[h, a, :, pl.ds(2 - 2 * zl, 2)], zbuf.at[i], zs.at[i], zr.at[i], z_side)

    def scatter_end(h):
        for a in range(2):
            i = (h, a)
            arrived(zbuf.at[i], zs.at[i], zr.at[i])
            for q in range(2):
                rows = slice(a * 64 + q * 32, a * 64 + q * 32 + 32)
                agg[h, :, rows, :] = x2[h, a, q, pl.ds(2 * zl, 2)] + zbuf[h, a, q]

    def weight_start(h):
        turned = dot(agg[h, 0], feat_ref[:128]) + dot(agg[h, 1], feat_ref[128:])
        local[h] = turned.T.reshape(32, 8, 128)

        @pl.loop(1, 32)
        def _(j):
            to = (me + j) % 32
            copy_to(local.at[h, to], a1.at[h, me], w1s.at[h], w1r.at[h], plane(to)).start()

        a1[h, me] = local[h, me]

    def taken(buffer, sem, h):
        count = buffer.shape[1] - 1
        ref = buffer.at[h, pl.ds(0, count)]
        pltpu.make_async_copy(ref, ref, sem.at[h]).wait()

    def weight_sum(h):
        taken(a1, w1r, h)
        part[h] = jnp.sum(a1[h], axis=0)

        @pl.loop(1, 8)
        def _(j):
            copy_to(part.at[h], a2.at[h, mz], w2s.at[h], w2r.at[h], column((mz + j) % 8)).start()

        a2[h, mz] = part[h]

    def weight_spread(h):
        taken(a2, w2r, h)
        mine = gw_ref.at[pl.ds(me * 8, 8), pl.ds(h * 128, 128)]
        mine[...] = jnp.sum(a2[h], axis=0) * (1.0 / math.sqrt(65536))

        @pl.loop(1, 32)
        def _(j):
            copy_to(mine, mine, w3s.at[h], w3r.at[h], plane((me + j) % 32)).start()

    def weight_end(h):
        taken(a1, w3r, h)

    def step(name, *calls):
        with jax.named_scope(name):
            for call, *args in calls:
                call(*args)

    def clear():
        runs[0] = jnp.zeros((128, 128), F32)

    def wait_loads():
        for copy in loads:
            copy.wait()

    def features_gradient():
        for t in range(2):
            turned = dot(weight_ref[:, :128], agg[0, t]) + dot(weight_ref[:, 128:], agg[1, t])
            gf_ref[t * 128:(t + 1) * 128, :] = turned.T

    def wait_sends():
        for copy in started:
            copy.wait_send()
        for h in range(2):
            taken(a1, w1s, h)
            taken(a2, w2s, h)
            taken(a1, w3s, h)

    step("gather_own_0", (gather_own, 0))
    step("sort_tiles", (sort_tiles,), (clear,))
    step("gather_next_0", (gather_next, 0))
    step("gather_own_1", (gather_own, 1), (wait_loads,))
    step("gather_last_0", (gather_last, 0))
    step("products_0", (products, 0))
    step("scatter_start_0", (scatter_start, 0), (scatter_direct, 0))
    step("gather_next_1", (gather_next, 1))
    step("gather_last_1", (gather_last, 1))
    step("products_1", (products, 1))
    step("scatter_ring_0", (scatter_ring, 0))
    step("scatter_start_1", (scatter_start, 1), (scatter_direct, 1))
    for p in range(4):
        step("scatter_cross_0_%d" % p, (scatter_cross, 0, p))
    step("scatter_cross_ring_0", (scatter_cross_ring, 0))
    step("scatter_ring_1", (scatter_ring, 1))
    step("scatter_z_0", (scatter_z, 0))
    step("scatter_end_0", (scatter_end, 0))
    step("weight_start_0", (weight_start, 0))
    for p in range(3):
        step("scatter_cross_1_%d" % p, (scatter_cross, 1, p))
    step("weight_sum_0", (weight_sum, 0))
    step("scatter_cross_ring_1", (scatter_cross_ring, 1))
    step("scatter_cross_1_3", (scatter_cross, 1, 3))
    step("weight_spread_0", (weight_spread, 0))
    step("scatter_z_1", (scatter_z, 1))
    step("scatter_end_1", (scatter_end, 1))
    step("weight_start_1", (weight_start, 1))
    step("features_gradient", (weight_end, 0), (features_gradient,))
    step("weight_sum_1", (weight_sum, 1))
    step("weight_spread_1", (weight_spread, 1))
    step("weight_end_1", (weight_end, 1))
    step("wait_sends", (wait_sends,))


def on_device(features, pre_act, upstream, weight, tile_vals, tile_row, tile_col, tile_count):
    dma = pltpu.SemaphoreType.DMA
    square = jax.ShapeDtypeStruct((256, 256), F32)
    piece = (4, 32, 128)
    vmem = pl.BlockSpec(memory_space=pltpu.VMEM)
    return pl.pallas_call(
        kernel,
        out_shape=(square, square),
        in_specs=[vmem] * 6
        + [pl.BlockSpec(memory_space=pltpu.SMEM), pl.BlockSpec(memory_space=pl.ANY)],
        out_specs=(vmem, vmem),
        scratch_shapes=[
            pltpu.VMEM((SLOTS, 128, 128), F32),
            pltpu.VMEM((SLOTS + 1, 128, 128), F32),
            pltpu.VMEM((16, 128, 256), BF16),
            pltpu.VMEM((2, 16, 128, 128), F32),
            pltpu.VMEM((2, 4, 4, 4, 128, 128), F32),
            pltpu.VMEM((2, 2, 2, 4) + piece, F32),
            pltpu.VMEM((2, 2, 2, 4) + piece, F32),
            pltpu.VMEM((2, 2, 2, 4) + piece, F32),
            pltpu.VMEM((2, 2, 4, 2) + piece, F32),
            pltpu.VMEM((2, 2, 2) + piece, F32),
            pltpu.VMEM((2, 2, 2) + piece, F32),
            pltpu.VMEM((2, 2, 2) + piece, F32),
            pltpu.VMEM((2, 2, 2) + piece, F32),
            pltpu.VMEM((2, 2, 2, 2, 32, 128), F32),
            pltpu.VMEM((2, 2, 128, 128), F32),
            pltpu.VMEM((2, 32, 8, 128), F32),
            pltpu.VMEM((2, 32, 8, 128), F32),
            pltpu.VMEM((2, 8, 128), F32),
            pltpu.VMEM((2, 8, 8, 128), F32),
            pltpu.VMEM((8, 256), jnp.int32),
            pltpu.VMEM((8, 256), jnp.int32),
            pltpu.SMEM((8, 256), jnp.int32),
            dma((LOADS,)),
            dma,
            dma((2, 14)),
            dma((2, 14)),
        ]
        + [dma((2, 2, 2, 4))] * 6
        + [dma((2, 2, 2))] * 6
        + [dma((2, 2))] * 2
        + [dma((2,))] * 6,
        compiler_params=pltpu.CompilerParams(
            collective_id=0, has_side_effects=True, vmem_limit_bytes=56 << 20
        ),
        name="layer",
    )(
        pre_act, upstream, features, weight,
        tile_row.reshape(1, SLOTS), tile_col.reshape(1, SLOTS), tile_count, tile_vals,
    )


def solution(mesh):
    return jax.shard_map(
        on_device,
        mesh=mesh,
        in_specs=(
            P(("row", "col"), None),
            P(("row", "col"), None),
            P(("row", "col"), None),
            P(),
            P(("row", "col"), None, None),
            P(("row", "col")),
            P(("row", "col")),
            P(("row", "col")),
        ),
        out_specs=(P(("row", "col"), None), P()),
        check_vma=False,
    )
```

time: 649 us -> 115 us (0.18)
  waiting for transfers between devices: 485 us -> 0 us
  Pallas kernels: 0 us -> 110 us
  other arithmetic: 56.1 us -> 0 us
  matrix products: 51 us -> 0 us
  local copies, waits for them, and re-layouts: 40.7 us -> 3.34 us
  between operations: 14.4 us -> 1.29 us
    psum x1 -> x0, waiting for transfers between devices: 264 us -> none  [on_device(): summed_grad = lax.psum(local_grad, ('row', 'col'))]
    reduce_scatter x1 -> x0, waiting for transfers between devices: 181 us -> none  [on_device(): lax.psum_scatter(partial_value, 'row', scatter_dimension=0, tiled=True)]
    pallas_call x0 -> x1, Pallas kernels: none -> 110 us  [on_device(): pl.pallas_call(kernel, out_shape=(square, square), in_specs=[vmem] * 6 +...]
    scatter-add x1 -> x0, other arithmetic: 52.6 us -> none  [on_device(): jax.ops.segment_sum(products, tile_col, num_segments=col_tiles)]
    dot_general x3 -> x0, matrix products: 51 us -> none  [the longest x1 46.7 us: on_device(): jnp.einsum('kab,kaf->kbf', tile_vals, picked, precision=lax.Precision.HIG...]
    all_gather x1 -> x0, waiting for transfers between devices: 40.7 us -> none  [on_device(): gathered = lax.all_gather(grad_pre, 'col', axis=0, tiled=True)]
    mul x1 -> x0, local copies, waits for them, and re-layouts: 22.4 us -> none  [on_device(): products = products * live_slots.astype(jnp.float32)[:, None, None]]
    gather x1 -> x0, local copies, waits for them, and re-layouts: 13.1 us -> none  [on_device(): picked = blocks[tile_row]]
  transfers between devices with their start and end apart: 3 -> 0, of which waited for: 3 -> 0; matrix products, arithmetic and copies ran while one was open for 0% -> 0% of each run, Pallas kernels for 0% -> 0%
where the time goes in v2:
time: 115 us; the launch traced here: 114 us
  Pallas kernels  110 us (96%)
  local copies, waits for them, and re-layouts  3.34 us (3%)
  between operations  1.29 us (1%)
    pallas_call x1, Pallas kernels, on_device(): pl.pallas_call(kernel, out_shape=(square, square), in_specs=[vmem] * 6 +...  110 us
    unnamed x2, local copies, waits for them, and re-layouts  3.34 us

profile of v2, /device:TPU:1, one launch (start us, length us, event | category | flops | bytes accessed | tf_op | source)
XLA Modules:
  0.0 114.4 jit_solution(11363398705499392823)
XLA Ops:
  1.3 109.8 %layer.1 = (f32[256,256]{1,0:T(8,128)}, f32[256,256]{1,0:T(8,128)}) custom-call(f32[256,256]{1,0:T(8,128)} %pre_ref.1, f32[256,256]{1,0:T(8,128)} %up_ref.1, f32[256,256]{1,0:T(8,128)} %feat_ref.1, f32[256,256]{1,0:T(8,128)} %weight_ref.1, s32[1,170]{1,0:T(1,128)} %bitcast.2, s32[1,170]{1,0:T(1,128)} %bitcast.3, s32[1]{0:T(128)S(6)} %copy.12.count_ref, ...), custom_call_target="tpu_custom_call" | custom-call | tf_op jit(solution)/shard_map/layer/pallas_call | solution.py:386
  111.0 1.7 %copy.13 = f32[256,256]{1,0:T(8,128)} copy(f32[256,256]{1,0:T(8,128)} %get-tuple-element.4) | data formatting | bytes 524288
  112.7 1.7 %copy.14 = f32[256,256]{1,0:T(8,128)} copy(f32[256,256]{1,0:T(8,128)} %get-tuple-element.5) | data formatting | bytes 524288

commit v3 on v2

--- a/solution.py
+++ b/solution.py
@@ -44,9 +44,9 @@
 def kernel(
     pre_ref, up_ref, feat_ref, weight_ref, row_ref, col_ref, count_ref, tiles_hbm,
     gf_ref, gw_ref,
-    tiles, runs, parts, gt, sums, r1, r2a, r2b, x1, s1, s2a, s2b, x2, zbuf, agg, local, a1, part, a2,
+    tiles, runs, parts, gt, sums, r1, r2a, r2b, x1, s1, s2a, s2b, x2, zbuf, fz, agg, local, a1, part, a2,
     raw, table_v, table,
-    load_sem, table_sem, ag_s, ag_r, r1s, r1r, r2as, r2ar, r2bs, r2br, s1s, s1r, s2as, s2ar, s2bs, s2br, zs, zr,
+    load_sem, table_sem, fzs, fzr, ag_s, ag_r, r1s, r1r, r2as, r2ar, r2bs, r2br, s1s, s1r, s2as, s2ar, s2bs, s2br, zs, zr,
     w1s, w1r, w2s, w2r, w3s, w3r,
 ):
     x, y, zl, zh, core = place()
@@ -54,21 +54,24 @@
     mz = zh * 2 + zl
     here = zh * 4 + core * 2
 
-    def plane(j):
-        return device(j // 8, (j // 2) % 4, zl, zh, j % 2)
-
-    def column(j):
-        return device(x, y, j % 2, j // 2, core)
+    xs, ys, zhs = ([(v + d) % 4 for d in range(4)] for v in (x, y, zh))
+    cores, zls = (core, 1 - core), (zl, 1 - zl)
+    near = sorted(
+        ((dx, dy, dc) for dx in range(4) for dy in range(4) for dc in range(2)),
+        key=lambda d: -(d[0] % 2 + d[0] // 2 * 2 - d[0] // 3 * 2 + d[1] % 2 + d[1] // 2 * 2 - d[1] // 3 * 2),
+    )
+    plane = [
+        (xs[dx] * 8 + ys[dy] * 2 + cores[dc], device(xs[dx], ys[dy], zl, zh, cores[dc]))
+        for dx, dy, dc in near
+        if (dx, dy, dc) != (0, 0, 0)
+    ]
+    column = [
+        device(x, y, zls[dl], zhs[dh], core) for dh in (2, 1, 3, 0) for dl in (1, 0) if (dh, dl) != (0, 0)
+    ]
 
     barrier = pltpu.get_barrier_semaphore()
-
-    @pl.loop(1, 32)
-    def _(j):
-        pl.semaphore_signal(barrier, inc=1, device_id=plane((me + j) % 32), device_id_type=MESH)
-
-    @pl.loop(1, 8)
-    def _(j):
-        pl.semaphore_signal(barrier, inc=1, device_id=column((mz + j) % 8), device_id_type=MESH)
+    for peer in column + [peer for _, peer in plane]:
+        pl.semaphore_signal(barrier, inc=1, device_id=peer, device_id_type=MESH)
 
     per_load = SLOTS // LOADS
     loads = []
@@ -163,7 +166,7 @@
             return jnp.minimum(jnp.maximum(value, 0), last)
 
         values = raw[...]
-        cols = jnp.where(lane < count_ref[0], values[0:1], 64)
+        cols = jnp.where(lane < count_ref[...], values[0:1], 64)
         key = cols * 256 + lane
         rank = down(total(jnp.where(down(key[0:1]) < key[0:1], one, none)))
         col_down, row_down = down(cols[0:1]), down(values[1:2])
@@ -268,27 +271,30 @@
                 arrived(s2a.at[i], s2as.at[i], s2ar.at[i])
                 arrived(s2b.at[i], s2bs.at[i], s2br.at[i])
             for q in range(2):
-                x2[h, a, q] = x1[h, a, 3, q] + s2b[h, a, q] + s2a[h, a, 1 - q]
+                rows = slice(a * 64 + q * 32, a * 64 + q * 32 + 32)
+                x2[h, :, rows, :] = x1[h, a, 3, q] + s2b[h, a, q] + s2a[h, a, 1 - q]
             i = (h, a)
-            go(x2.at[h, a, :, pl.ds(2 - 2 * zl, 2)], zbuf.at[i], zs.at[i], zr.at[i], z_side)
+            rows = pl.ds(a * 64, 64)
+            go(x2.at[h, pl.ds(2 - 2 * zl, 2), rows, :], zbuf.at[h, :, rows, :], zs.at[i], zr.at[i], z_side)
 
     def scatter_end(h):
         for a in range(2):
             i = (h, a)
-            arrived(zbuf.at[i], zs.at[i], zr.at[i])
-            for q in range(2):
-                rows = slice(a * 64 + q * 32, a * 64 + q * 32 + 32)
-                agg[h, :, rows, :] = x2[h, a, q, pl.ds(2 * zl, 2)] + zbuf[h, a, q]
+            arrived(zbuf.at[h, :, pl.ds(a * 64, 64), :], zs.at[i], zr.at[i])
+        agg[h] = x2[h, pl.ds(2 * zl, 2)] + zbuf[h]
+
+    def features_send():
+        go(feat_ref, fz, fzs, fzr, z_side)
+
+    def features_wait():
+        arrived(fz, fzs, fzr)
 
     def weight_start(h):
-        turned = dot(agg[h, 0], feat_ref[:128]) + dot(agg[h, 1], feat_ref[128:])
+        turned = dot(x2[h, 2 * zl], feat_ref[:128]) + dot(x2[h, 2 * zl + 1], feat_ref[128:])
+        turned += dot(x2[h, 2 - 2 * zl], fz[:128]) + dot(x2[h, 3 - 2 * zl], fz[128:])
         local[h] = turned.T.reshape(32, 8, 128)
-
-        @pl.loop(1, 32)
-        def _(j):
-            to = (me + j) % 32
-            copy_to(local.at[h, to], a1.at[h, me], w1s.at[h], w1r.at[h], plane(to)).start()
-
+        for to, peer in plane:
+            copy_to(local.at[h, to], a1.at[h, me], w1s.at[h], w1r.at[h], peer).start()
         a1[h, me] = local[h, me]
 
     def taken(buffer, sem, h):
@@ -299,21 +305,16 @@
     def weight_sum(h):
         taken(a1, w1r, h)
         part[h] = jnp.sum(a1[h], axis=0)
-
-        @pl.loop(1, 8)
-        def _(j):
-            copy_to(part.at[h], a2.at[h, mz], w2s.at[h], w2r.at[h], column((mz + j) % 8)).start()
-
+        for peer in column:
+            copy_to(part.at[h], a2.at[h, mz], w2s.at[h], w2r.at[h], peer).start()
         a2[h, mz] = part[h]
 
     def weight_spread(h):
         taken(a2, w2r, h)
         mine = gw_ref.at[pl.ds(me * 8, 8), pl.ds(h * 128, 128)]
         mine[...] = jnp.sum(a2[h], axis=0) * (1.0 / math.sqrt(65536))
-
-        @pl.loop(1, 32)
-        def _(j):
-            copy_to(mine, mine, w3s.at[h], w3r.at[h], plane((me + j) % 32)).start()
+        for _, peer in plane:
+            copy_to(mine, mine, w3s.at[h], w3r.at[h], peer).start()
 
     def weight_end(h):
         taken(a1, w3r, h)
@@ -346,12 +347,14 @@
     step("gather_own_0", (gather_own, 0))
     step("sort_tiles", (sort_tiles,), (clear,))
     step("gather_next_0", (gather_next, 0))
-    step("gather_own_1", (gather_own, 1), (wait_loads,))
+    step("gather_own_1", (gather_own, 1))
+    step("loads", (wait_loads,))
     step("gather_last_0", (gather_last, 0))
     step("products_0", (products, 0))
     step("scatter_start_0", (scatter_start, 0), (scatter_direct, 0))
     step("gather_next_1", (gather_next, 1))
     step("gather_last_1", (gather_last, 1))
+    step("weight_features_send", (features_send,))
     step("products_1", (products, 1))
     step("scatter_ring_0", (scatter_ring, 0))
     step("scatter_start_1", (scatter_start, 1), (scatter_direct, 1))
@@ -360,21 +363,21 @@
     step("scatter_cross_ring_0", (scatter_cross_ring, 0))
     step("scatter_ring_1", (scatter_ring, 1))
     step("scatter_z_0", (scatter_z, 0))
-    step("scatter_end_0", (scatter_end, 0))
-    step("weight_start_0", (weight_start, 0))
+    step("weight_start_0", (features_wait,), (weight_start, 0))
     for p in range(3):
         step("scatter_cross_1_%d" % p, (scatter_cross, 1, p))
-    step("weight_sum_0", (weight_sum, 0))
     step("scatter_cross_ring_1", (scatter_cross_ring, 1))
     step("scatter_cross_1_3", (scatter_cross, 1, 3))
+    step("weight_sum_0", (weight_sum, 0))
+    step("scatter_z_1", (scatter_z, 1))
+    step("weight_start_1", (weight_start, 1))
     step("weight_spread_0", (weight_spread, 0))
-    step("scatter_z_1", (scatter_z, 1))
+    step("scatter_end_0", (scatter_end, 0))
     step("scatter_end_1", (scatter_end, 1))
-    step("weight_start_1", (weight_start, 1))
-    step("features_gradient", (weight_end, 0), (features_gradient,))
+    step("features_gradient", (features_gradient,))
     step("weight_sum_1", (weight_sum, 1))
     step("weight_spread_1", (weight_spread, 1))
-    step("weight_end_1", (weight_end, 1))
+    step("weight_end_1", (weight_end, 0), (weight_end, 1))
     step("wait_sends", (wait_sends,))
 
 
@@ -386,8 +389,7 @@
     return pl.pallas_call(
         kernel,
         out_shape=(square, square),
-        in_specs=[vmem] * 6
-        + [pl.BlockSpec(memory_space=pltpu.SMEM), pl.BlockSpec(memory_space=pl.ANY)],
+        in_specs=[vmem] * 7 + [pl.BlockSpec(memory_space=pl.ANY)],
         out_specs=(vmem, vmem),
         scratch_shapes=[
             pltpu.VMEM((SLOTS, 128, 128), F32),
@@ -402,8 +404,9 @@
             pltpu.VMEM((2, 2, 2) + piece, F32),
             pltpu.VMEM((2, 2, 2) + piece, F32),
             pltpu.VMEM((2, 2, 2) + piece, F32),
-            pltpu.VMEM((2, 2, 2) + piece, F32),
-            pltpu.VMEM((2, 2, 2, 2, 32, 128), F32),
+            pltpu.VMEM((2, 4, 128, 128), F32),
+            pltpu.VMEM((2, 2, 128, 128), F32),
+            pltpu.VMEM((256, 256), F32),
             pltpu.VMEM((2, 2, 128, 128), F32),
             pltpu.VMEM((2, 32, 8, 128), F32),
             pltpu.VMEM((2, 32, 8, 128), F32),
@@ -414,6 +417,8 @@
             pltpu.SMEM((8, 256), jnp.int32),
             dma((LOADS,)),
             dma,
+            dma,
+            dma,
             dma((2, 14)),
             dma((2, 14)),
         ]
@@ -422,12 +427,12 @@
         + [dma((2, 2))] * 2
         + [dma((2,))] * 6,
         compiler_params=pltpu.CompilerParams(
-            collective_id=0, has_side_effects=True, vmem_limit_bytes=56 << 20
+            collective_id=0, has_side_effects=True, vmem_limit_bytes=48 << 20
         ),
         name="layer",
     )(
         pre_act, upstream, features, weight,
-        tile_row.reshape(1, SLOTS), tile_col.reshape(1, SLOTS), tile_count, tile_vals,
+        tile_row.reshape(1, SLOTS), tile_col.reshape(1, SLOTS), tile_count.reshape(1, 1), tile_vals,
     )
 
 

time: 115 us -> 106 us (0.922)
  Pallas kernels: 110 us -> 98.1 us
  local copies, waits for them, and re-layouts: 3.34 us -> 6.56 us
    pallas_call x1, Pallas kernels: 110 us -> 98.1 us  [on_device(): pl.pallas_call(kernel, out_shape=(square, square), in_specs=[vmem] * 7 +...]
    unnamed x2 -> x14, local copies, waits for them, and re-layouts: 3.34 us -> 6.56 us
where the time goes in v3:
time: 106 us
  Pallas kernels  98.1 us (93%)
  local copies, waits for them, and re-layouts  6.56 us (6%)
  between operations  1.3 us (1%)
    pallas_call x1, Pallas kernels, on_device(): pl.pallas_call(kernel, out_shape=(square, square), in_specs=[vmem] * 7 +...  98.1 us
    unnamed x14, local copies, waits for them, and re-layouts  6.56 us

profile of v3, /device:TPU:1, one launch (start us, length us, event | category | flops | bytes accessed | tf_op | source)
XLA Modules:
  0.0 105.9 jit_solution(14487078370138356281)
XLA Ops:
  1.3 0.0 copy-start
  1.3 0.9 copy-done
  2.2 0.0 copy-start.1
  2.2 0.9 copy-done.1
  3.2 0.0 copy-start.2
  3.2 0.9 copy-done.2
  4.1 0.0 copy-start.3
  4.1 0.9 copy-done.3
  5.1 0.0 copy-start.4
  5.1 0.7 copy-done.4
  5.8 0.0 copy-start.5
  5.8 0.7 copy-done.5
  6.4 98.1 %layer.1 = (f32[256,256]{1,0:T(8,128)S(1)}, f32[256,256]{1,0:T(8,128)S(1)}) custom-call(f32[256,256]{1,0:T(8,128)S(1)} %copy-done, f32[256,256]{1,0:T(8,128)S(1)} %copy-done.1, f32[256,256]{1,0:T(8,128)S(1)} %copy-done.2, f32[256,256]{1,0:T(8,128)S(1)} %copy-done.3, s32[1,170]{1,0:T(1,128)S(1)} %bitcast.4, s32[1,170]{1,0:T(1,128)S(1)} %bitcast.5, ...), custom_call_target="tpu_custom_call" | custom-call | tf_op jit(solution)/shard_map/layer/pallas_call | solution.py:389
  104.5 0.7 copy.13
  105.2 0.7 copy.14
Async XLA Ops:
  1.3 1.0 copy-start
  2.2 0.9 copy-start.1
  3.2 0.9 copy-start.2
  4.1 0.9 copy-start.3
  5.1 0.7 copy-start.4
  5.8 0.7 copy-start.5

commit v4 on v0

v4 whole, which is shorter than its diff:
```python
import math

import jax
import jax.numpy as jnp
from jax import lax
from jax.experimental import pallas as pl
from jax.experimental.pallas import tpu as pltpu
from jax.sharding import PartitionSpec as P

MESH = pl.DeviceIdType.MESH
HIGH = lax.Precision.HIGHEST
F32 = jnp.float32
BF16 = jnp.bfloat16
SLOTS = 170
UNROLL = 34
LOADS = 10


def place():
    row = lax.axis_index("row")
    col = lax.axis_index("col")
    return row // 8, (row // 2) % 4, row % 2, col // 2, col % 2


def device(x, y, zl, zh, core):
    return (x * 8 + y * 2 + zl, zh * 2 + core)


def copy_to(src, dst, send, recv, target):
    return pltpu.make_async_remote_copy(
        src_ref=src, dst_ref=dst, send_sem=send, recv_sem=recv, device_id=target, device_id_type=MESH
    )


def split(value):
    high = value.astype(BF16)
    return high, (value - high.astype(F32)).astype(BF16)


def dot(a, b):
    return jnp.dot(a, b, precision=HIGH, preferred_element_type=F32)


PARTS = ((0, 128), (128, 128))
SIDE = (48, 64)
REST = 32


def kernel(pre_hbm, up_hbm, feat_hbm, weight_hbm, row_hbm, col_hbm, count_hbm, tiles_hbm, gf_ref, gw_ref, ref, sem):
    x, y, zl, zh, core = place()
    me = x * 8 + y * 2 + core
    mz = zh * 2 + zl
    here = zh * 4 + core * 2

    loaded = {}

    def load(name, src, dst, slot):
        loaded[name] = pltpu.make_async_copy(src, dst, sem["in"].at[slot])
        loaded[name].start()

    load("pre", pre_hbm, ref["pre"], 0)
    load("up", up_hbm, ref["up"], 1)

    xs, ys, zhs = ([(v + d) % 4 for d in range(4)] for v in (x, y, zh))
    cores, zls = (core, 1 - core), (zl, 1 - zl)
    hops = (0, 1, 2, 1)
    offsets = [(dx, dy, dc) for dx in range(4) for dy in range(4) for dc in range(2) if dx + dy + dc]
    offsets.sort(key=lambda d: -hops[d[0]] - hops[d[1]])
    plane = [
        (xs[dx] * 8 + ys[dy] * 2 + cores[dc], device(xs[dx], ys[dy], zl, zh, cores[dc])) for dx, dy, dc in offsets
    ]
    column = [
        device(x, y, zls[dl], zhs[dh], core) for dh in (2, 1, 3, 0) for dl in (1, 0) if (dh, dl) != (0, 0)
    ]

    barrier = pltpu.get_barrier_semaphore()
    for peer in column + [peer for _, peer in plane]:
        pl.semaphore_signal(barrier, inc=1, device_id=peer, device_id_type=MESH)

    load("row", row_hbm, ref["row"], 2)
    load("col", col_hbm, ref["col"], 3)
    load("count", count_hbm, ref["count"], 4)
    per_load = SLOTS // LOADS
    for i in range(LOADS):
        rows = pl.ds(i * per_load, per_load)
        load(i, tiles_hbm.at[rows], ref["tiles"].at[rows], 7 + i)
    load("feat", feat_hbm, ref["feat"], 5)
    load("weight", weight_hbm, ref["weight"], 6)

    loaded["pre"].wait()
    loaded["up"].wait()
    pre = ref["pre"][...]
    gate = jax.nn.sigmoid(pre)
    grad = ref["up"][...] * gate * (1.0 + pre * (1.0 - gate))
    for t in range(2):
        turned = grad[t * 128:(t + 1) * 128, :].T
        for h, (low, size) in enumerate(PARTS):
            ref["gt"][h][here + t] = turned[low:low + size]
    pl.semaphore_wait(barrier, 38)

    started = []

    def go(src, dst, send, recv, target):
        copy = copy_to(src, dst, send, recv, target)
        copy.start()
        started.append(copy)

    z_right = device(x, y, zl, zhs[1], core)
    z_left = device(x, y, zl, zhs[3], core)
    sibling = device(x, y, zl, zh, 1 - core)
    z_side = device(x, y, 1 - zl, zh, core)
    x_side = (device(xs[1], y, zl, zh, core), device(xs[3], y, zl, zh, core))
    y_side = (device(x, ys[1], zl, zh, core), device(x, ys[3], zl, zh, core))

    def arrived(dst, send, recv):
        copy_to(dst, dst, send, recv, z_side).wait_recv()

    after, before, far = zhs[1], zhs[3], zhs[2]

    def block(h, block_zh, block_core, half):
        rows = PARTS[h][1] // 2
        return ref["gt"][h].at[pl.ds(block_zh * 4 + block_core * 2, 2), pl.ds(half * rows, rows), :]

    def pass_on(h, block_zh, half, slot, target):
        this = block(h, block_zh, core, half)
        go(this, this, sem["ag_s"].at[h, slot], sem["ag_r"].at[h, slot], target)

    def came(h, block_zh, block_core, half, slot):
        arrived(block(h, block_zh, block_core, half), sem["ag_s"].at[h, slot], sem["ag_r"].at[h, slot])

    def gather_own(h):
        pass_on(h, zh, 0, 0, z_right)
        pass_on(h, zh, 1, 3, z_left)
        pass_on(h, zh, 1, 1, z_right)
        pass_on(h, zh, 0, 2, z_left)
        pass_on(h, zh, 0, 6, sibling)
        pass_on(h, zh, 1, 7, sibling)

    def gather_next(h):
        came(h, before, core, 0, 0)
        pass_on(h, before, 0, 4, z_right)
        came(h, after, core, 1, 3)
        pass_on(h, after, 1, 5, z_left)
        pass_on(h, before, 0, 8, sibling)
        pass_on(h, after, 1, 9, sibling)

    def gather_rest(h):
        came(h, before, core, 1, 1)
        pass_on(h, before, 1, 10, sibling)
        came(h, after, core, 0, 2)
        pass_on(h, after, 0, 11, sibling)

    def gather_last(h):
        came(h, far, core, 0, 4)
        pass_on(h, far, 0, 12, sibling)
        came(h, far, core, 1, 5)
        pass_on(h, far, 1, 13, sibling)
        blocks = ((zh, 0), (zh, 1), (before, 0), (after, 1), (before, 1), (after, 0), (far, 0), (far, 1))
        for i, (block_zh, half) in enumerate(blocks):
            came(h, block_zh, 1 - core, half, 6 + i)

    def sort_tiles():
        raw, table_v = ref["raw"], ref["table_v"]
        for name in ("row", "col", "count"):
            loaded[name].wait()
        raw[...] = jnp.zeros((8, 256), jnp.int32)
        raw[0:1, 0:SLOTS] = ref["col"][...]
        raw[1:2, 0:SLOTS] = ref["row"][...]
        lane = lax.broadcasted_iota(jnp.int32, (8, 256), 1)
        across = lax.broadcasted_iota(jnp.int32, (256, 256), 1)
        slot_down = lax.broadcasted_iota(jnp.int32, (256, 1), 0)
        one, none = jnp.int32(1), jnp.int32(0)

        def down(value):
            return jnp.broadcast_to(value, (8, 256)).T[:, 0:1]

        def total(value):
            return jnp.sum(value, axis=0, keepdims=True)

        def within(value, last):
            return jnp.minimum(jnp.maximum(value, 0), last)

        values = raw[...]
        cols = jnp.where(lane < ref["count"][...], values[0:1], 64)
        key = cols * 256 + lane
        rank = down(total(jnp.where(down(key[0:1]) < key[0:1], one, none)))
        col_down, row_down = down(cols[0:1]), down(values[1:2])
        at = rank == across
        next_at = rank + 1 == across
        sorted_cols = total(jnp.where(at, col_down, 0))
        previous = total(jnp.where(next_at, col_down + 1, 0)) - 1
        table_v[0:1] = within(total(jnp.where(at, slot_down, 0)), SLOTS - 1)
        table_v[1:2] = within(total(jnp.where(at, row_down, 0)), 15)
        table_v[2:3] = jnp.where(sorted_cols == previous, one, none)
        table_v[3:4] = within(total(jnp.where(col_down <= across, one, none)), SLOTS)
        table_v[4:5] = jnp.where(total(jnp.where(col_down == across, one, none)) > 0, one, none)
        table_v[5:8] = jnp.zeros((3, 256), jnp.int32)
        copy = pltpu.make_async_copy(table_v, ref["table"], sem["table"])
        copy.start()
        copy.wait()
        ref["runs"][0] = jnp.zeros((128, 128), F32)

    def wait_tiles():
        for i in range(LOADS):
            loaded[i].wait()

    def split_part(h):
        size = PARTS[h][1]

        @pl.loop(0, 16)
        def _(i):
            high, low = split(ref["gt"][h][i])
            ref["bits"][i, :size, :128] = high
            ref["bits"][i, :size, 128:] = low

    def products(h, begin, end):
        size = PARTS[h][1]
        runs, table = ref["runs"], ref["table"]

        @pl.loop(begin, end)
        def _(i):
            for j in range(UNROLL):
                k = i * UNROLL + j
                high, low = split(ref["tiles"][table[0, k]])
                both = jnp.concatenate([high, low], axis=1)
                both = jnp.concatenate([both, both], axis=0)
                product = jnp.dot(ref["bits"][table[1, k], :size, :], both, preferred_element_type=F32)
                carried = table[2, k].astype(F32) * runs[k, :size, :]
                runs[k + 1, :size, :] = carried + product[:, :128] + product[:, 128:]

    def column_sums(h):
        size = PARTS[h][1]
        runs, table = ref["runs"], ref["table"]

        @pl.loop(0, 16)
        def _(i):
            for j in range(4):
                t = i * 4 + j
                ref["sums"][h][i // 4, i % 4, j] = table[4, t].astype(F32) * runs[table[3, t], :size, :]

    first, second = (x_side, y_side), (y_side, x_side)
    c1, c2 = (xs, ys), (ys, xs)
    order = (2, 1, 3, 0)
    ahead = (1, 3)
    sides = tuple((a, d) for a in range(2) for d in range(2))

    def piece(h, a, d1, p, q):
        quarter = SIDE[h] // 2
        d1, d2 = c1[a][d1], c2[a][order[p]]
        rows = pl.ds((a * 2 + q) * quarter, quarter)
        sums = ref["sums"][h]
        return sums.at[d1, d2, :, rows, :] if a == 0 else sums.at[d2, d1, :, rows, :]

    def sent(h, name, i, src, target):
        go(src, ref[name][h].at[i], sem[name + "s"].at[(h,) + i], sem[name + "r"].at[(h,) + i], target)

    def got(h, name, i):
        arrived(ref[name][h].at[i], sem[name + "s"].at[(h,) + i], sem[name + "r"].at[(h,) + i])
        return ref[name][h][i]

    def scatter_start(h):
        for p in range(4):
            for a, d in sides:
                sent(h, "r1", (a, d, p), piece(h, a, 2, p, d), first[a][d])

    def scatter_direct(h):
        for p in range(4):
            for a, d in sides:
                sent(h, "r2a", (a, d, p), piece(h, a, ahead[d], p, 1 - d), first[a][d])

    def scatter_ring(h):
        for p in range(4):
            for a, d in sides:
                i = (a, d, p)
                ref["r1"][h][i] = got(h, "r1", i) + piece(h, a, ahead[d], p, d)[...]
                sent(h, "r2b", i, ref["r1"][h].at[i], first[a][d])

    def scatter_cross(h, p):
        x1 = ref["x1"][h]
        for a in range(2):
            direct = [got(h, "r2a", (a, d, p)) for d in range(2)]
            around = [got(h, "r2b", (a, d, p)) for d in range(2)]
            for q in range(2):
                x1[a, p, q] = piece(h, a, 0, p, q)[...] + around[q] + direct[1 - q]
            if p == 0:
                for d in range(2):
                    sent(h, "s1", (a, d), x1.at[a, 0, d], second[a][d])
            elif p < 3:
                sent(h, "s2a", (a, p - 1), x1.at[a, p, 2 - p], second[a][p - 1])

    def scatter_cross_ring(h):
        x1 = ref["x1"][h]
        for p in (1, 2):
            for a in range(2):
                i = (a, p - 1)
                x1[a, p, p - 1] += got(h, "s1", i)
                sent(h, "s2b", i, x1.at[a, p, p - 1], second[a][p - 1])

    def z_refs(h, a, part):
        rows = pl.ds(a * SIDE[h], SIDE[h])
        return ref["x2"].at[h, pl.ds(part, 2), rows, :], ref["zbuf"].at[h, :, rows, :]

    def scatter_z(h):
        for a in range(2):
            direct = [got(h, "s2a", (a, d)) for d in range(2)]
            around = [got(h, "s2b", (a, d)) for d in range(2)]
            for q in range(2):
                rows = slice((2 * a + q) * SIDE[h] // 2, (2 * a + q + 1) * SIDE[h] // 2)
                ref["x2"][h, :, rows, :] = ref["x1"][h][a, 3, q] + around[q] + direct[1 - q]
            src, dst = z_refs(h, a, 2 - 2 * zl)
            go(src, dst, sem["zs"].at[h, a], sem["zr"].at[h, a], z_side)

    def scatter_end():
        for h in range(len(PARTS)):
            for a in range(2):
                arrived(z_refs(h, a, 0)[1], sem["zs"].at[h, a], sem["zr"].at[h, a])
        for g in range(2):
            ref["agg"][g] = ref["x2"][g, pl.ds(2 * zl, 2)] + ref["zbuf"][g]

    opposite = (device(x, ys[2], zl, zh, core), device(xs[2], y, zl, zh, core))

    def rest_send(h):
        for i in range(4):
            src = ref["sums"][h].at[i, :, pl.ds(2 - 2 * zl, 2), pl.ds(2 * SIDE[h], REST), :]
            sent(h, "rest", (i,), src, z_side)

    def rest_piece(h, a, d1, q):
        d1 = c1[a][d1]
        rows = pl.ds((a * 2 + q) * (REST // 4), REST // 4)
        rest = ref["rest"][h]
        return rest.at[d1, :, :, rows, :] if a == 0 else rest.at[:, d1, :, rows, :]

    def rest_start(h):
        for i in range(4):
            own = ref["sums"][h][i, :, pl.ds(2 * zl, 2), 2 * SIDE[h]:, :]
            ref["rest"][h][i] = got(h, "rest", (i,)) + own
        for a, d in sides:
            sent(h, "y1", (a, d), rest_piece(h, a, 2, d), first[a][d])
        for a, d in sides:
            sent(h, "y2a", (a, d), rest_piece(h, a, ahead[d], 1 - d), first[a][d])

    def rest_ring(h):
        for a, d in sides:
            ref["y1"][h][a, d] = got(h, "y1", (a, d)) + rest_piece(h, a, ahead[d], d)[...]
            sent(h, "y2b", (a, d), ref["y1"][h].at[a, d], first[a][d])

    def rest_cross(h):
        y3 = ref["y3"][h]
        for a in range(2):
            direct = [got(h, "y2a", (a, d)) for d in range(2)]
            around = [got(h, "y2b", (a, d)) for d in range(2)]
            for q in range(2):
                y3[a, q] = rest_piece(h, a, 0, q)[...] + around[q] + direct[1 - q]
            for p, target in enumerate((opposite[a], second[a][0], second[a][1])):
                sent(h, "y4", (a, p), y3.at[a, :, c2[a][order[p]]], target)

    def rest_end(h):
        for a in range(2):
            mine = ref["y3"][h][a, :, c2[a][0]]
            for p in range(3):
                mine += got(h, "y4", (a, p))
            for q in range(2):
                begin = 2 * SIDE[h] + (a * 2 + q) * (REST // 4)
                rows = slice(begin, begin + REST // 4)
                ref["x2"][h, pl.ds(2 * zl, 2), rows, :] = mine[q]
        none = jnp.zeros((2, REST, 128), F32)
        ref["x2"][h, pl.ds(2 - 2 * zl, 2), 2 * SIDE[h]:, :] = none
        ref["zbuf"][h, :, 2 * SIDE[h]:, :] = none

    def features_send():
        loaded["feat"].wait()
        go(ref["feat"], ref["fz"], sem["fzs"], sem["fzr"], z_side)

    def features_wait():
        arrived(ref["fz"], sem["fzs"], sem["fzr"])
        for name, zp in (("feat", zl), ("fz", 1 - zl)):
            rows = pl.ds(pl.multiple_of(zp * 256, 256), 256)
            ref["feat_high"][rows, :], ref["feat_low"][rows, :] = split(ref[name][...])

    def weight_start(g):
        x2, local = ref["x2"], ref["local"]
        high, low = split(jnp.concatenate([x2[g, i] for i in range(4)], axis=1))
        turned = sum(
            jnp.dot(a, ref[b][...], preferred_element_type=F32)
            for a, b in ((low, "feat_high"), (high, "feat_low"), (high, "feat_high"))
        )
        local[g] = turned.T.reshape(32, 8, 128)
        for to, peer in plane:
            copy_to(local.at[g, to], ref["a1"].at[g, me], sem["w1s"].at[g], sem["w1r"].at[g], peer).start()
        ref["a1"][g, me] = local[g, me]

    def taken(name, which, g):
        count = ref[name].shape[1] - 1
        some = ref[name].at[g, pl.ds(0, count)]
        pltpu.make_async_copy(some, some, sem[which].at[g]).wait()

    def weight_sum(g):
        taken("a1", "w1r", g)
        ref["part"][g] = jnp.sum(ref["a1"][g], axis=0)
        for peer in column:
            copy_to(ref["part"].at[g], ref["a2"].at[g, mz], sem["w2s"].at[g], sem["w2r"].at[g], peer).start()
        ref["a2"][g, mz] = ref["part"][g]

    def weight_spread(g):
        taken("a2", "w2r", g)
        mine = gw_ref.at[pl.ds(me * 8, 8), pl.ds(g * 128, 128)]
        mine[...] = jnp.sum(ref["a2"][g], axis=0) * (1.0 / math.sqrt(65536))
        for _, peer in plane:
            copy_to(mine, mine, sem["w3s"].at[g], sem["w3r"].at[g], peer).start()

    def weight_end():
        for g in range(2):
            taken("a1", "w3r", g)

    def features_gradient():
        agg, weight = ref["agg"], ref["weight"]
        loaded["weight"].wait()
        for t in range(2):
            turned = dot(weight[:, :128], agg[0, t]) + dot(weight[:, 128:], agg[1, t])
            gf_ref[t * 128:(t + 1) * 128, :] = turned.T

    def wait_sends():
        for copy in started:
            copy.wait_send()
        for g in range(2):
            taken("a1", "w1s", g)
            taken("a2", "w2s", g)
            taken("a1", "w3s", g)

    def cross(h, *places):
        for p in places:
            scatter_cross(h, p)

    chunks = SLOTS // UNROLL
    gather_own(0)
    sort_tiles()
    gather_next(0)
    gather_own(1)
    gather_rest(0)
    wait_tiles()
    gather_last(0)
    split_part(0)
    products(0, 0, 3)
    gather_next(1)
    products(0, 3, chunks)
    column_sums(0)
    scatter_start(0)
    scatter_direct(0)
    gather_rest(1)
    gather_last(1)
    rest_send(0)
    split_part(1)
    products(1, 0, 1)
    scatter_ring(0)
    products(1, 1, chunks)
    cross(0, 0, 1)
    column_sums(1)
    scatter_start(1)
    scatter_direct(1)
    features_send()
    cross(0, 2, 3)
    scatter_cross_ring(0)
    rest_start(0)
    scatter_ring(1)
    scatter_z(0)
    rest_ring(0)
    features_wait()
    cross(1, 0, 1)
    rest_cross(0)
    cross(1, 2)
    scatter_cross_ring(1)
    rest_end(0)
    weight_start(0)
    cross(1, 3)
    scatter_z(1)
    weight_start(1)
    weight_sum(0)
    scatter_end()
    features_gradient()
    weight_sum(1)
    weight_spread(0)
    weight_spread(1)
    weight_end()
    wait_sends()


def deliver(gf_ref, gw_ref, gf_out, gw_out):
    gf_out[...] = gf_ref[...]
    gw_out[...] = gw_ref[...]


def on_device(features, pre_act, upstream, weight, tile_vals, tile_row, tile_col, tile_count):
    dma = pltpu.SemaphoreType.DMA
    square = jax.ShapeDtypeStruct((256, 256), F32)
    count = len(PARTS)

    def f32(*shape):
        return pltpu.VMEM(shape, F32)

    def i32(*shape):
        return pltpu.VMEM(shape, jnp.int32)

    def pieces(*lead):
        return [f32(*lead, 4, side // 2, 128) for side in SIDE]

    def rests(*lead):
        return [f32(*lead, REST // 4, 128)]

    ref = dict(
        pre=f32(256, 256), up=f32(256, 256), feat=f32(256, 256), weight=f32(256, 256), fz=f32(256, 256),
        row=i32(1, SLOTS), col=i32(1, SLOTS), count=i32(1, 1), raw=i32(8, 256), table_v=i32(8, 256),
        table=pltpu.SMEM((8, 256), jnp.int32),
        tiles=f32(SLOTS, 128, 128),
        runs=f32(SLOTS + 1, 128, 128),
        bits=pltpu.VMEM((16, 128, 256), BF16),
        gt=[f32(16, size, 128) for _, size in PARTS],
        sums=[f32(4, 4, 4, size, 128) for _, size in PARTS],
        r1=pieces(2, 2, 4), r2a=pieces(2, 2, 4), r2b=pieces(2, 2, 4), x1=pieces(2, 4, 2),
        s1=pieces(2, 2), s2a=pieces(2, 2), s2b=pieces(2, 2),
        rest=[f32(4, 4, 2, REST, 128)],
        y1=rests(2, 2, 4, 2), y2a=rests(2, 2, 4, 2), y2b=rests(2, 2, 4, 2), y3=rests(2, 2, 4, 2), y4=rests(2, 3, 2, 2),
        feat_high=pltpu.VMEM((512, 256), BF16), feat_low=pltpu.VMEM((512, 256), BF16),
        x2=f32(2, 4, 128, 128), zbuf=f32(2, 2, 128, 128), agg=f32(2, 2, 128, 128),
        local=f32(2, 32, 8, 128), a1=f32(2, 32, 8, 128), part=f32(2, 8, 128), a2=f32(2, 8, 8, 128),
    )
    sem = {"in": dma((7 + LOADS,)), "table": dma, "fzs": dma, "fzr": dma}
    for side in "sr":
        sem["ag_" + side] = dma((count, 14))
        for name in ("r1", "r2a", "r2b"):
            sem[name + side] = dma((count, 2, 2, 4))
        for name in ("s1", "s2a", "s2b", "y1", "y2a", "y2b"):
            sem[name + side] = dma((count, 2, 2))
        sem["rest" + side] = dma((count, 4))
        sem["y4" + side] = dma((count, 2, 3))
        sem["z" + side] = dma((count, 2))
        for name in ("w1", "w2", "w3"):
            sem[name + side] = dma((2,))
    vmem = pl.BlockSpec(memory_space=pltpu.VMEM)
    hbm = pl.BlockSpec(memory_space=pltpu.HBM)
    results = pl.pallas_call(
        kernel,
        out_shape=(square, square),
        in_specs=[hbm] * 8,
        out_specs=(vmem, vmem),
        scratch_shapes=[ref, sem],
        compiler_params=pltpu.CompilerParams(
            collective_id=0, has_side_effects=True, vmem_limit_bytes=56 << 20
        ),
        name="layer",
    )(
        pre_act, upstream, features, weight,
        tile_row.reshape(1, SLOTS), tile_col.reshape(1, SLOTS), tile_count.reshape(1, 1), tile_vals,
    )
    return pl.pallas_call(
        deliver,
        out_shape=(square, square),
        in_specs=[vmem] * 2,
        out_specs=(vmem,) * 2,
        name="deliver",
    )(*results)


def solution(mesh):
    return jax.shard_map(
        on_device,
        mesh=mesh,
        in_specs=(
            P(("row", "col"), None),
            P(("row", "col"), None),
            P(("row", "col"), None),
            P(),
            P(("row", "col"), None, None),
            P(("row", "col")),
            P(("row", "col")),
            P(("row", "col")),
        ),
        out_specs=(P(("row", "col"), None), P()),
        check_vma=False,
    )
```

time: 649 us -> 98.1 us (0.15)
  waiting for transfers between devices: 485 us -> 0 us
  Pallas kernels: 0 us -> 96.7 us
  other arithmetic: 56.1 us -> 0 us
  matrix products: 51 us -> 0 us
  local copies, waits for them, and re-layouts: 40.7 us -> 0 us
  between operations: 14.4 us -> 1.29 us
    psum x1 -> x0, waiting for transfers between devices: 264 us -> none  [on_device(): summed_grad = lax.psum(local_grad, ('row', 'col'))]
    reduce_scatter x1 -> x0, waiting for transfers between devices: 181 us -> none  [on_device(): lax.psum_scatter(partial_value, 'row', scatter_dimension=0, tiled=True)]
    pallas_call x0 -> x2, Pallas kernels: none -> 96.7 us  [the longest x1 94.8 us: on_device(): pl.pallas_call(kernel, out_shape=(square, square), in_specs=[hbm] * 8, ou...]
    scatter-add x1 -> x0, other arithmetic: 52.6 us -> none  [on_device(): jax.ops.segment_sum(products, tile_col, num_segments=col_tiles)]
    dot_general x3 -> x0, matrix products: 51 us -> none  [the longest x1 46.7 us: on_device(): jnp.einsum('kab,kaf->kbf', tile_vals, picked, precision=lax.Precision.HIG...]
    all_gather x1 -> x0, waiting for transfers between devices: 40.7 us -> none  [on_device(): gathered = lax.all_gather(grad_pre, 'col', axis=0, tiled=True)]
    mul x1 -> x0, local copies, waits for them, and re-layouts: 22.4 us -> none  [on_device(): products = products * live_slots.astype(jnp.float32)[:, None, None]]
    gather x1 -> x0, local copies, waits for them, and re-layouts: 13.1 us -> none  [on_device(): picked = blocks[tile_row]]
  transfers between devices with their start and end apart: 3 -> 0, of which waited for: 3 -> 0; matrix products, arithmetic and copies ran while one was open for 0% -> 0% of each run, Pallas kernels for 0% -> 0%
where the time goes in v4:
time: 98.1 us; the launch traced here: 98 us
  Pallas kernels  96.7 us (99%)
  between operations  1.29 us (1%)
    pallas_call x1, Pallas kernels, on_device(): pl.pallas_call(kernel, out_shape=(square, square), in_specs=[hbm] * 8, ou...  94.8 us

profile of v4, /device:TPU:1, one launch (start us, length us, event | category | flops | bytes accessed | tf_op | source)
XLA Modules:
  0.0 98.0 jit_solution(5488061143947518147)
XLA Ops:
  1.3 94.8 %layer.1 = (f32[256,256]{1,0:T(8,128)}, f32[256,256]{1,0:T(8,128)}) custom-call(f32[256,256]{1,0:T(8,128)} %pre_hbm.1, f32[256,256]{1,0:T(8,128)} %up_hbm.1, f32[256,256]{1,0:T(8,128)} %feat_hbm.1, f32[256,256]{1,0:T(8,128)} %weight_hbm.1, s32[1,170]{1,0:T(1,128)} %bitcast.4, s32[1,170]{1,0:T(1,128)} %bitcast.5, s32[1,1]{1,0:T(1,128)} %bitcast.3.count_hbm, ...), custom_call_target="tpu_custom_call" | custom-call | tf_op jit(solution)/shard_map/layer/pallas_call | solution.py:540
  96.1 1.8 %deliver.1 = (f32[256,256]{1,0:T(8,128)}, f32[256,256]{1,0:T(8,128)}) custom-call(f32[256,256]{1,0:T(8,128)} %get-tuple-element.4.gf_ref, f32[256,256]{1,0:T(8,128)} %get-tuple-element.5.gw_ref), custom_call_target="tpu_custom_call" | custom-call | tf_op jit(solution)/shard_map/deliver/pallas_call | solution.py:554

commit v5 on v4

--- a/solution.py
+++ b/solution.py
@@ -460,15 +460,15 @@
     features_send()
     cross(0, 2, 3)
     scatter_cross_ring(0)
-    rest_start(0)
     scatter_ring(1)
     scatter_z(0)
+    rest_start(0)
+    cross(1, 0, 1)
     rest_ring(0)
-    features_wait()
-    cross(1, 0, 1)
-    rest_cross(0)
     cross(1, 2)
     scatter_cross_ring(1)
+    rest_cross(0)
+    features_wait()
     rest_end(0)
     weight_start(0)
     cross(1, 3)
@@ -484,14 +484,8 @@
     wait_sends()
 
 
-def deliver(gf_ref, gw_ref, gf_out, gw_out):
-    gf_out[...] = gf_ref[...]
-    gw_out[...] = gw_ref[...]
-
-
 def on_device(features, pre_act, upstream, weight, tile_vals, tile_row, tile_col, tile_count):
     dma = pltpu.SemaphoreType.DMA
-    square = jax.ShapeDtypeStruct((256, 256), F32)
     count = len(PARTS)
 
     def f32(*shape):
@@ -537,9 +531,9 @@
             sem[name + side] = dma((2,))
     vmem = pl.BlockSpec(memory_space=pltpu.VMEM)
     hbm = pl.BlockSpec(memory_space=pltpu.HBM)
-    results = pl.pallas_call(
+    return pl.pallas_call(
         kernel,
-        out_shape=(square, square),
+        out_shape=(f32(256, 256), f32(256, 256)),
         in_specs=[hbm] * 8,
         out_specs=(vmem, vmem),
         scratch_shapes=[ref, sem],
@@ -551,13 +545,6 @@
         pre_act, upstream, features, weight,
         tile_row.reshape(1, SLOTS), tile_col.reshape(1, SLOTS), tile_count.reshape(1, 1), tile_vals,
     )
-    return pl.pallas_call(
-        deliver,
-        out_shape=(square, square),
-        in_specs=[vmem] * 2,
-        out_specs=(vmem,) * 2,
-        name="deliver",
-    )(*results)
 
 
 def solution(mesh):

time: 98.1 us -> 96.9 us (0.988)
  Pallas kernels: 96.7 us -> 94.1 us
  local copies, waits for them, and re-layouts: 0 us -> 1.41 us
    pallas_call x2 -> x1, Pallas kernels: 96.7 us -> 94.1 us  [on_device(): pl.pallas_call(kernel, out_shape=(f32(256, 256), f32(256, 256)), in_specs...]
    unnamed x0 -> x2, local copies, waits for them, and re-layouts: none -> 1.41 us
where the time goes in v5:
time: 96.9 us; the launch traced here: 96.8 us
  Pallas kernels  94.1 us (97%)
  local copies, waits for them, and re-layouts  1.41 us (1%)
  between operations  1.29 us (1%)
    pallas_call x1, Pallas kernels, on_device(): pl.pallas_call(kernel, out_shape=(f32(256, 256), f32(256, 256)), in_specs...  94.1 us

profile of v5, /device:TPU:1, one launch (start us, length us, event | category | flops | bytes accessed | tf_op | source)
XLA Modules:
  0.0 96.8 jit_solution(3014297575872763253)
XLA Ops:
  1.3 94.1 %layer.1 = (f32[256,256]{1,0:T(8,128)S(1)}, f32[256,256]{1,0:T(8,128)S(1)}) custom-call(f32[256,256]{1,0:T(8,128)} %pre_hbm.1, f32[256,256]{1,0:T(8,128)} %up_hbm.1, f32[256,256]{1,0:T(8,128)} %feat_hbm.1, f32[256,256]{1,0:T(8,128)} %weight_hbm.1, s32[1,170]{1,0:T(1,128)} %bitcast.4, s32[1,170]{1,0:T(1,128)} %bitcast.5, s32[1,1]{1,0:T(1,128)} %bitcast.3.count_hbm, ...), custom_call_target="tpu_custom_call" | custom-call | tf_op jit(solution)/shard_map/layer/pallas_call | solution.py:534
  95.4 0.7 copy.12
  96.1 0.7 copy.13
